TPU v7x, 32 devices: a whole 2x2x4 slice. The times are simulated.
32 devices in a mesh: groups: 2 (over x), tok: 8 (over z, y), dom: 2 (over core).
Axes of the slice: x: 2, y: 2, z: 4, core: 2. Of those that a mesh axis runs over, the one named last changes fastest.
Arguments:
- states: bfloat16 [32, 128, 768], P(('groups', 'dom'), 'tok'), parts along dimension 0, may hold values from -12 to 12
- ancestors: int32 [32], P(('groups', 'dom')), parts along dimension 0, may hold values from 0 to 15, as said below
- noise: bfloat16 [32, 128, 768], P(('groups', 'dom'), 'tok'), parts along dimension 0, may hold values from -6 to 6
- pair: bfloat16 [256, 128, 128], P(('groups', 'tok')), parts along dimension 0, may hold values from -200 to 200
- token_mask: int32 [256], P('groups'), parts along dimension 0, may hold values 0 or 1
- w_qkv: bfloat16 [2, 768, 2304], replicated, may hold values from -0.21875 to 0.21875
- w_out: bfloat16 [2, 768, 768], replicated, may hold values from -0.21875 to 0.21875
- w_pair: bfloat16 [2, 128, 16], replicated, may hold values from -1.5 to 1.5
Outputs:
- new_states: bfloat16 [32, 128, 768], P(('groups', 'dom'), 'tok'), parts along dimension 0
There are 2 independent parts, one for each index of `groups`. A program takes and returns all parts, laid end to end along the dimension named above; an argument that names none is the same for every part. Nothing has to cross between parts.
Inputs may be any that keep to these rules, and one draw needn't show every extreme that they name: `ancestors`: nondecreasing over particles; the first entry is 0 and the last is 15.
All inputs are finite; a program needn't handle non-finite values.
Results may differ from a plain program's by a relative error of at most 0.015.
Values may be sent and summed in bfloat16 or wider, within the bound.
A program may use at most 128 MiB of HBM per device.

v0:
```python
import functools

import jax
import jax.numpy as jnp
from jax import lax
from jax.experimental import pallas as pl
from jax.experimental.pallas import tpu as pltpu
from jax.sharding import PartitionSpec as P


def layer_norm(stream):
    values = stream.astype(jnp.float32)
    average = jnp.mean(values, axis=-1, keepdims=True)
    centred = values - average
    spread = jnp.mean(centred * centred, axis=-1, keepdims=True)
    return centred * lax.rsqrt(spread + 1e-05)


def token_split_body(states, ancestors, noise, pair, token_mask, w_qkv, w_out, w_pair):
    part_count = states.shape[0]
    tok_rows = states.shape[1]
    model_width = states.shape[2]
    head_count = w_pair.shape[2]
    head_width = model_width // head_count
    layer_count = w_qkv.shape[0]
    total_keys = pair.shape[1]
    everyone = lax.all_gather(states, "dom", axis=0, tiled=True)
    chosen = jnp.take(everyone, ancestors, axis=0)
    stream = (chosen.astype(jnp.float32) + 0.5 * noise.astype(jnp.float32)).astype(jnp.bfloat16)
    penalty = jnp.where(token_mask > 0, 0.0, -1000000000.0).astype(jnp.float32)
    pair_terms = jnp.einsum("ijc,lch->lhij", pair, w_pair, preferred_element_type=jnp.float32)
    full_bias = pair_terms + penalty[None, None, None, :]
    query_scale = head_width ** (-0.5)
    for layer_index in range(layer_count):
        normed = layer_norm(stream).astype(jnp.bfloat16)
        projected = jnp.dot(
            normed.reshape(part_count * tok_rows, model_width),
            w_qkv[layer_index],
            preferred_element_type=jnp.float32,
        )
        projected = projected.reshape(part_count, tok_rows, 3 * model_width)
        query = (projected[..., :model_width] * query_scale).astype(jnp.bfloat16)
        key_tiles = projected[..., model_width : 2 * model_width].astype(jnp.bfloat16)
        value_tiles = projected[..., 2 * model_width :].astype(jnp.bfloat16)
        layer_bias = full_bias[layer_index]
        query_heads = query.reshape(part_count, tok_rows, head_count, head_width)
        all_keys, all_values = (
            lax.all_gather(key_tiles, "tok", axis=1, tiled=True),
            lax.all_gather(value_tiles, "tok", axis=1, tiled=True),
        )
        key_heads = all_keys.reshape(part_count, total_keys, head_count, head_width)
        scores = (
            jnp.einsum(
                "pihe,pjhe->phij", query_heads, key_heads, preferred_element_type=jnp.float32
            )
            + layer_bias[None]
        )
        weights = jax.nn.softmax(scores, axis=-1).astype(jnp.bfloat16)
        value_heads = all_values.reshape(part_count, total_keys, head_count, head_width)
        attended = jnp.einsum(
            "phij,pjhe->pihe", weights, value_heads, preferred_element_type=jnp.float32
        ).astype(jnp.bfloat16)
        attended = attended.reshape(part_count * tok_rows, model_width)
        update = jnp.dot(attended, w_out[layer_index], preferred_element_type=jnp.float32)
        update = update.reshape(part_count, tok_rows, model_width)
        stream = (stream.astype(jnp.float32) + update).astype(jnp.bfloat16)
    return stream


MESH = pl.DeviceIdType.MESH
LANES = 128


def particle_kernel(
    peers,
    head_count,
    ancestors_hbm,
    states,
    noise_hbm,
    pair_hbm,
    mask_hbm,
    w_pair_hbm,
    w_qkv_hbm,
    w_out_hbm,
    result,
    ancestors,
    noise,
    pair,
    token_mask,
    w_pair,
    everyone,
    outgoing,
    stream_in,
    bias,
    bias_rows,
    qkv,
    score_rows,
    raised,
    finished,
    w_qkv,
    w_out,
    load_sem,
    weight_sem,
    state_sem,
    stream_send,
    stream_recv,
    bias_send,
    bias_recv,
    relay_send,
    relay_recv,
    out_send,
    out_recv,
):
    group = lax.axis_index("groups")
    me = lax.axis_index("tok")
    core = lax.axis_index("dom")
    sibling = (group, me, 1 - core)
    part_count, tok_rows, width = states.shape
    layer_count = w_qkv.shape[0]
    tokens = peers * tok_rows
    head_width = width // head_count
    half_heads = head_count // 2

    def ahead(step):
        return lax.rem(me + step, peers)

    def behind(step):
        return lax.rem(me + peers - step, peers)

    half = peers // 2
    side, place_in_half = me // half, lax.rem(me, half)
    far = [
        (half + step, (1 - side) * half + lax.rem(place_in_half + step, half))
        for step in range(half)
    ]
    near = [
        (step, side * half + lax.rem(place_in_half + step, half)) for step in range(1, half)
    ]
    exchanges = near + far

    def remote(source, target, send, recv, device):
        return pltpu.make_async_remote_copy(
            src_ref=source,
            dst_ref=target,
            send_sem=send,
            recv_sem=recv,
            device_id=device,
            device_id_type=MESH,
        )

    weight_copies = []
    for layer in range(layer_count):
        weight_copies.append(
            (
                pltpu.make_async_copy(w_qkv_hbm.at[layer], w_qkv.at[layer], weight_sem.at[layer, 0]),
                pltpu.make_async_copy(w_out_hbm.at[layer], w_out.at[layer], weight_sem.at[layer, 1]),
            )
        )
    mine = pl.ds(core * part_count, part_count)
    loads = []
    for place, (source, target) in enumerate(
        (
            (pair_hbm, pair),
            (w_pair_hbm, w_pair),
            (mask_hbm, token_mask),
            (ancestors_hbm, ancestors),
            (states, everyone.at[mine]),
            (noise_hbm, noise),
        )
    ):
        loads.append(pltpu.make_async_copy(source, target, load_sem.at[place]))
        loads[-1].start()
    weight_copies[0][0].start()

    barrier = pltpu.get_barrier_semaphore()
    pl.semaphore_signal(barrier, inc=1, device_id=sibling, device_id_type=MESH)
    for step in range(1, peers):
        pl.semaphore_signal(
            barrier, inc=1, device_id=(group, ahead(step), core), device_id_type=MESH
        )
    pl.semaphore_wait(barrier, peers)

    state_copies = []
    share = part_count // 2
    for piece in range(2):
        copy = remote(
            states.at[pl.ds(piece * share, share)],
            everyone.at[pl.ds(core * part_count + piece * share, share)],
            state_sem.at[0, piece],
            state_sem.at[1, piece],
            sibling,
        )
        copy.start()
        state_copies.append(copy)
    def make_bias(layer):
        penalty = jnp.where(token_mask[...] > 0, 0.0, -1000000000.0).astype(jnp.float32)
        pair_terms = lax.dot_general(
            w_pair[layer],
            pair[...].reshape(tok_rows * tokens, pair.shape[2]),
            (((1,), (1,)), ((), ())),
            preferred_element_type=jnp.float32,
        )
        for row in range(tok_rows):
            full = pair_terms[:, row * tokens : (row + 1) * tokens] + penalty
            bias_rows[:, row, :] = full - jnp.max(full, axis=-1, keepdims=True)
        bias[layer, me] = bias_rows[...].astype(jnp.bfloat16)

    my_heads = pl.ds(core * half_heads, half_heads)
    pairs = peers // 2
    partner = me + 1 - 2 * lax.rem(me, 2)
    bias_copies = []

    def send_bias(layer, slot, owner, target):
        block = bias.at[layer, owner, my_heads]
        copy = remote(
            block,
            block,
            bias_send.at[layer, slot],
            bias_recv.at[layer, slot],
            (group, target, core),
        )
        copy.start()
        bias_copies.append(copy)
        return copy

    def spread(layer):
        copies = [send_bias(layer, 0, me, partner)]
        for step in range(1, pairs):
            copies.append(send_bias(layer, step, me, ahead(2 * step)))
        return copies

    def hand_over(layer, slot, owner):
        block = bias.at[layer, owner, my_heads]
        copy = remote(
            block, block, relay_send.at[layer, slot], relay_recv.at[layer, slot], sibling
        )
        copy.start()
        return copy

    def relay_own_parity(layer, copies):
        handed = []
        for step in range(1, pairs):
            copies[step].wait_recv()
            copies.append(send_bias(layer, pairs - 1 + step, behind(2 * step), partner))
            handed.append(hand_over(layer, step, behind(2 * step)))
        copies[0].wait_recv()
        handed.append(hand_over(layer, 0, partner))
        return handed

    def relay_partner(layer, copies):
        handed = []
        for step in range(1, pairs):
            slot = pairs - 1 + step
            copies[slot].wait_recv()
            owner = lax.rem(partner + peers - 2 * step, peers)
            handed.append(hand_over(layer, slot, owner))
        return handed

    for load in loads[:3]:
        load.wait()
    make_bias(0)
    spreads = [spread(0)]
    relays = []

    for load in loads[3:]:
        load.wait()
    for copy in state_copies:
        copy.wait()

    def moved(particle):
        chosen = everyone[ancestors[particle]].astype(jnp.float32)
        return (chosen + 0.5 * noise[particle].astype(jnp.float32)).astype(jnp.bfloat16)

    stream_copies = []
    for step, target in exchanges:
        outgoing[step] = moved(target)
        copy = remote(
            outgoing.at[step],
            stream_in.at[me],
            stream_send.at[step],
            stream_recv.at[step],
            (group, target, core),
        )
        copy.start()
        stream_copies.append(copy)
    stream_in[me] = moved(me)
    for layer in range(layer_count):
        if layer > 0:
            weight_copies[layer][0].start()
        weight_copies[layer][1].start()

    for layer in range(1, layer_count):
        make_bias(layer)
    relays.append(relay_own_parity(0, spreads[0]))
    def head_lanes(head, start, size):
        lanes = lax.broadcasted_iota(jnp.int32, (1, size), 1) + start
        inside = (lanes >= head * head_width) & (lanes < (head + 1) * head_width)
        return jnp.where(inside, 1.0, 0.0).astype(jnp.bfloat16)

    def attend(layer, first_block, blocks, kept_rows):
        rows = blocks * tok_rows
        tiles = []
        ready = 0
        for tile in range(width // LANES):
            start = tile * LANES
            first = start // head_width
            last = (start + LANES + head_width - 1) // head_width
            for head in range(ready, last):
                first_score = pl.multiple_of(head * tokens + first_block * tok_rows, tok_rows)
                bias_block = bias[layer, pl.ds(first_block, blocks), head]
                scores = score_rows[pl.ds(first_score, rows)] + bias_block.reshape(
                    rows, tokens
                ).astype(jnp.float32)
                largest = jnp.max(scores, axis=-1, keepdims=True)
                raised[kept_rows, pl.ds(head * tokens, tokens)] = jnp.exp(scores - largest).astype(
                    jnp.bfloat16
                )
            ready = last
            value = qkv[:, pl.ds(2 * width + start, LANES)]
            masks = [
                jnp.broadcast_to(head_lanes(head, start, LANES), (tokens, LANES))
                for head in range(first, last)
            ]
            sides = jnp.concatenate(
                [jnp.concatenate([value * mask, mask], axis=1) for mask in masks], axis=0
            )
            part = jnp.dot(
                raised[kept_rows, pl.ds(first * tokens, (last - first) * tokens)],
                sides,
                preferred_element_type=jnp.float32,
            )
            tiles.append((part[:, :LANES] / part[:, LANES:]).astype(jnp.bfloat16))
        return jnp.concatenate(tiles, axis=1)

    def project(layer, first_block, blocks, attended):
        update = jnp.dot(attended, w_out[layer], preferred_element_type=jnp.float32)
        old = stream_in[pl.ds(first_block, blocks)].astype(jnp.float32)
        return (old + update.reshape(old.shape)).astype(jnp.bfloat16)

    def make_qkv(layer, first_block, blocks):
        rows = blocks * tok_rows
        first_row = first_block * tok_rows
        if blocks < peers:
            first_row = pl.multiple_of(first_row, rows)
        stream = stream_in[pl.ds(first_block, blocks)].reshape(rows, width)
        normed = layer_norm(stream).astype(jnp.bfloat16)
        for block in range(3):
            columns = pl.ds(block * width, width)
            projected = jnp.dot(
                normed, w_qkv[layer, :, columns], preferred_element_type=jnp.float32
            )
            if block == 0:
                projected = projected * head_width ** (-0.5)
            qkv[pl.ds(first_row, rows), columns] = projected.astype(jnp.bfloat16)

    windows = []
    for head in range(head_count):
        if windows and (head + 1) * head_width <= windows[-1][0] + 2 * LANES:
            windows[-1][1].append(head)
        else:
            start = head * head_width // LANES * LANES
            windows.append((min(start, width - 2 * LANES), [head]))

    for layer in range(layer_count):
        if layer == 0:
            for copy in stream_copies[: half - 1]:
                copy.wait_recv()
            weight_copies[0][0].wait()
            make_qkv(0, side * half, half)
            relays[0] += relay_partner(0, spreads[0])
            for copy in stream_copies[half - 1 :]:
                copy.wait_recv()
            if layer + 1 < layer_count:
                spreads.append(spread(layer + 1))
            make_qkv(0, (1 - side) * half, half)
        else:
            if layer + 1 < layer_count:
                spreads.append(spread(layer + 1))
            weight_copies[layer][0].wait()
            make_qkv(layer, 0, peers)
        for start, heads in windows:
            query = qkv[:, pl.ds(start, 2 * LANES)]
            score_rows[pl.ds(heads[0] * tokens, len(heads) * tokens)] = lax.dot_general(
                jnp.concatenate(
                    [query * head_lanes(head, start, 2 * LANES) for head in heads], axis=0
                ),
                qkv[:, pl.ds(width + start, 2 * LANES)],
                (((1,), (1,)), ((), ())),
                preferred_element_type=jnp.float32,
            )
        for copy in relays[layer]:
            copy.wait_recv()
        if layer + 1 < layer_count:
            relays.append(relay_own_parity(layer + 1, spreads[layer + 1]))
        if layer + 1 < layer_count:
            attended = attend(layer, 0, peers, pl.ds(0, tokens))
            relays[layer + 1] += relay_partner(layer + 1, spreads[layer + 1])
            weight_copies[layer][1].wait()
            stream_in[...] = project(layer, 0, peers, attended)

    last = layer_count - 1
    weight_copies[last][1].wait()
    out_copies = []
    for turn, (owner, exchange) in enumerate(((1 - side, far), (side, near))):
        first_block = owner * half
        kept_rows = pl.ds(turn * half * tok_rows, half * tok_rows)
        attended = attend(last, first_block, half, kept_rows)
        finished[pl.ds(first_block, half)] = project(last, first_block, half, attended)
        for slot, target in exchange:
            copy = remote(
                finished.at[target],
                result.at[me],
                out_send.at[slot],
                out_recv.at[slot],
                (group, target, core),
            )
            copy.start()
            out_copies.append(copy)
    kept = pltpu.make_async_copy(finished.at[me], result.at[me], load_sem.at[6])
    kept.start()
    for copies in [stream_copies, bias_copies] + relays:
        for copy in copies:
            copy.wait_send()
    for copy in out_copies:
        copy.wait()
    kept.wait()


def particle_body(peers, states, ancestors, noise, pair, token_mask, w_qkv, w_out, w_pair):
    part_count, tok_rows, width = states.shape
    layer_count, _, head_count = w_pair.shape
    tokens = peers * tok_rows
    hbm = pl.BlockSpec(memory_space=pltpu.HBM)
    dma = pltpu.SemaphoreType.DMA
    per_peer, per_layer = dma((peers,)), dma((layer_count, peers))
    return pl.pallas_call(
        functools.partial(particle_kernel, peers, head_count),
        out_shape=jax.ShapeDtypeStruct(states.shape, states.dtype),
        in_specs=[hbm] * 8,
        out_specs=hbm,
        scratch_shapes=[
            pltpu.SMEM(ancestors.shape, ancestors.dtype),
            pltpu.VMEM(noise.shape, noise.dtype),
            pltpu.VMEM(pair.shape, pair.dtype),
            pltpu.VMEM((1, tokens), token_mask.dtype),
            pltpu.VMEM((layer_count, head_count, w_pair.shape[1]), w_pair.dtype),
            pltpu.VMEM((2 * part_count, tok_rows, width), jnp.bfloat16),
            pltpu.VMEM((peers, tok_rows, width), jnp.bfloat16),
            pltpu.VMEM((peers, tok_rows, width), jnp.bfloat16),
            pltpu.VMEM((layer_count, peers, head_count, tok_rows, tokens), jnp.bfloat16),
            pltpu.VMEM((head_count, tok_rows, tokens), jnp.float32),
            pltpu.VMEM((tokens, 3 * width), jnp.bfloat16),
            pltpu.VMEM((head_count * tokens, tokens), jnp.float32),
            pltpu.VMEM((tokens, head_count * tokens), jnp.bfloat16),
            pltpu.VMEM((peers, tok_rows, width), jnp.bfloat16),
            pltpu.VMEM(w_qkv.shape, w_qkv.dtype),
            pltpu.VMEM(w_out.shape, w_out.dtype),
            dma((7,)),
            dma((layer_count, 2)),
            dma((2, 2)),
            per_peer,
            per_peer,
            per_layer,
            per_layer,
            per_layer,
            per_layer,
            per_peer,
            per_peer,
        ],
        compiler_params=pltpu.CompilerParams(
            collective_id=0, has_side_effects=True, vmem_limit_bytes=63 * 1024 * 1024
        ),
        name="particle_layers",
    )(
        ancestors,
        states,
        noise,
        pair,
        token_mask.reshape(1, tokens),
        jnp.transpose(w_pair, (0, 2, 1)),
        w_qkv,
        w_out,
    )


def body(peers, states, ancestors, noise, pair, token_mask, w_qkv, w_out, w_pair):
    part_count, tok_rows, width = states.shape
    one_each = part_count == peers and peers % 2 == 0 and tok_rows % 16 == 0 and peers * tok_rows == LANES and width % LANES == 0
    inner = functools.partial(particle_body, peers) if one_each else token_split_body
    return inner(states, ancestors, noise, pair, token_mask, w_qkv, w_out, w_pair)


def solution(mesh):
    placed = (
        P(("groups", "dom"), "tok", None),
        P(("groups", "dom")),
        P(("groups", "dom"), "tok", None),
        P(("groups", "tok"), None, None),
        P("groups"),
        P(),
        P(),
        P(),
    )
    return jax.shard_map(
        functools.partial(body, mesh.shape["tok"]),
        mesh=mesh,
        in_specs=placed,
        out_specs=P(("groups", "dom"), "tok", None),
        check_vma=False,
    )
```

profile of v0, /device:TPU:0, one launch (start us, length us, event | category | flops | bytes accessed | tf_op | source)
XLA Modules:
  0.0 33.3 jit_solution(8501853511641543027)
XLA Ops:
  0.0 31.7 %particle_layers.1 = bf16[8,16,768]{2,1,0:T(8,128)(2,1)} custom-call(s32[8]{0:T(128)} %ancestors_hbm.1, bf16[8,16,768]{2,1,0:T(8,128)(2,1)} %states.1, bf16[8,16,768]{2,1,0:T(8,128)(2,1)} %noise_hbm.1, bf16[16,128,128]{2,1,0:T(8,128)(2,1)} %pair_hbm.1, s32[1,128]{1,0:T(1,128)} %bitcast.3, bf16[2,16,128]{2,1,0:T(8,128)(2,1)} %bitcast.2, ...), custom_call_target="tpu_custom_call" | custom-call | tf_op jit(solution)/shard_map/particle_layers/pallas_call | solution.py:436
  31.7 1.6 %copy.10 = bf16[8,16,768]{2,1,0:T(8,128)(2,1)} copy(bf16[8,16,768]{2,1,0:T(8,128)(2,1)} %particle_layers.1) | data formatting | bytes 393216
where the time goes:
time: 33.5 us; the launch traced here: 33.3 us
  Pallas kernels  31.7 us (95%)
  local copies, waits for them, and re-layouts  1.62 us (5%)
    pallas_call x1, Pallas kernels, particle_body(): pl.pallas_call(functools.partial(particle_kernel, peers, head_count), out...  31.7 us
    unnamed x1, local copies, waits for them, and re-layouts  1.62 us

commit v1 on v0

--- a/solution.py
+++ b/solution.py
@@ -178,6 +178,16 @@
         pl.semaphore_signal(
             barrier, inc=1, device_id=(group, ahead(step), core), device_id_type=MESH
         )
+    def pair_product(layer):
+        return lax.dot_general(
+            w_pair[layer],
+            pair[...].reshape(tok_rows * tokens, pair.shape[2]),
+            (((1,), (1,)), ((), ())),
+            preferred_element_type=jnp.float32,
+        )
+    for load in loads[:3]:
+        load.wait()
+    first_terms = pair_product(0)
     pl.semaphore_wait(barrier, peers)
 
     state_copies = []
@@ -192,14 +202,8 @@
         )
         copy.start()
         state_copies.append(copy)
-    def make_bias(layer):
+    def make_bias(layer, pair_terms):
         penalty = jnp.where(token_mask[...] > 0, 0.0, -1000000000.0).astype(jnp.float32)
-        pair_terms = lax.dot_general(
-            w_pair[layer],
-            pair[...].reshape(tok_rows * tokens, pair.shape[2]),
-            (((1,), (1,)), ((), ())),
-            preferred_element_type=jnp.float32,
-        )
         for row in range(tok_rows):
             full = pair_terms[:, row * tokens : (row + 1) * tokens] + penalty
             bias_rows[:, row, :] = full - jnp.max(full, axis=-1, keepdims=True)
@@ -256,9 +260,7 @@
             handed.append(hand_over(layer, slot, owner))
         return handed
 
-    for load in loads[:3]:
-        load.wait()
-    make_bias(0)
+    make_bias(0, first_terms)
     spreads = [spread(0)]
     relays = []
 
@@ -290,7 +292,7 @@
         weight_copies[layer][1].start()
 
     for layer in range(1, layer_count):
-        make_bias(layer)
+        make_bias(layer, pair_product(layer))
     relays.append(relay_own_parity(0, spreads[0]))
     def head_lanes(head, start, size):
         lanes = lax.broadcasted_iota(jnp.int32, (1, size), 1) + start

time: 33.5 us -> 33.3 us (level)
  no operation moved by 1% of the time
where the time goes in v1:
time: 33.3 us; the launch traced here: 33.1 us
  Pallas kernels  31.5 us (95%)
  local copies, waits for them, and re-layouts  1.62 us (5%)
    pallas_call x1, Pallas kernels, particle_body(): pl.pallas_call(functools.partial(particle_kernel, peers, head_count), out...  31.5 us
    unnamed x1, local copies, waits for them, and re-layouts  1.62 us

profile of v1, /device:TPU:0, one launch (start us, length us, event | category | flops | bytes accessed | tf_op | source)
XLA Modules:
  0.0 33.1 jit_solution(1819426912122001053)
XLA Ops:
  0.0 31.5 %particle_layers.1 = bf16[8,16,768]{2,1,0:T(8,128)(2,1)} custom-call(s32[8]{0:T(128)} %ancestors_hbm.1, bf16[8,16,768]{2,1,0:T(8,128)(2,1)} %states.1, bf16[8,16,768]{2,1,0:T(8,128)(2,1)} %noise_hbm.1, bf16[16,128,128]{2,1,0:T(8,128)(2,1)} %pair_hbm.1, s32[1,128]{1,0:T(1,128)} %bitcast.3, bf16[2,16,128]{2,1,0:T(8,128)(2,1)} %bitcast.2, ...), custom_call_target="tpu_custom_call" | custom-call | tf_op jit(solution)/shard_map/particle_layers/pallas_call | solution.py:438
  31.5 1.6 %copy.10 = bf16[8,16,768]{2,1,0:T(8,128)(2,1)} copy(bf16[8,16,768]{2,1,0:T(8,128)(2,1)} %particle_layers.1) | data formatting | bytes 393216
